TPU v7x, 128 devices: a whole 4x4x4 slice. The times are simulated.
128 devices in a mesh: dp: 2 (over x_lo), tm: 16 (over z, y), head: 4 (over x_hi, core).
Axes of the slice: x: 4 (x_hi: 2, x_lo: 2; x = x_hi * 2 + x_lo), y: 4, z: 4, core: 2. Of those that a mesh axis runs over, the one named last changes fastest.
Arguments:
- clip: bfloat16 [32, 1792, 1152], P(('dp', 'tm'), 'head'), parts along dimension 0, may hold values from -8 to 8
- modulation: float32 [12, 1152], P('dp'), parts along dimension 0, may hold values from -3 to 3
- w_qkv_s: bfloat16 [1152, 3456], replicated, may hold values from -1.9 to 1.9
- w_out_s: bfloat16 [1152, 1152], replicated, may hold values from -0.1875 to 0.1875
- w_qkv_t: bfloat16 [1152, 3456], replicated, may hold values from -1.9 to 1.9
- w_out_t: bfloat16 [1152, 1152], replicated, may hold values from -0.1875 to 0.1875
Outputs:
- result: bfloat16 [32, 1792, 1152], P(('dp', 'tm'), 'head'), parts along dimension 0
There are 2 independent parts, one for each index of `dp`. A program takes and returns all parts, laid end to end along the dimension named above; an argument that names none is the same for every part. Nothing has to cross between parts.
All inputs are finite; a program needn't handle non-finite values.
Results may differ from a plain program's by a relative error of at most 0.017.
Values may be sent and summed in bfloat16 or wider, within the bound.
No kernel may reach another device: no remote copies, remote signals or barrier semaphores. Data moves between devices by JAX's collectives and lax.ppermute only.
A program may use at most 192 MiB of HBM per device.

v0:
```python
import math

import jax
import jax.numpy as jnp
from jax import lax
from jax.experimental import pallas as pl
from jax.experimental.pallas import tpu as pltpu
from jax.sharding import PartitionSpec as P

HEADS = 16
HEAD_DIM = 72
WIDTH = 1152
ROWS = 448
QUERIES = 896
WINDOW = 640
HALF_COLS = 576
AUG = 80
PADDED = 512
LOOK = 2
QSCALE = math.log2(math.e) / math.sqrt(HEAD_DIM)
NT = (((1,), (1,)), ((), ()))
TN = (((0,), (0,)), ((), ()))
BF16 = jnp.bfloat16
F32 = jnp.float32
VMEM = pl.BlockSpec(memory_space=pltpu.VMEM)
SMEM = pl.BlockSpec(memory_space=pltpu.SMEM)
HBM = pl.BlockSpec(memory_space=pltpu.HBM)
EXCESS = 64.0


def params(mebibytes):
    return pltpu.CompilerParams(vmem_limit_bytes=mebibytes * 1024 * 1024)


def modulate(values, shift_vec, scale_vec):
    values = values.astype(F32)
    average = jnp.mean(values, axis=-1, keepdims=True)
    centred = values - average
    variance = jnp.mean(centred * centred, axis=-1, keepdims=True)
    normed = centred * lax.rsqrt(variance + 1e-06)
    return (normed * (1.0 + scale_vec) + shift_vec).astype(BF16)


def window_copy(w_hbm, third, core, place, sem):
    start = pl.multiple_of(third * WIDTH + core * 512, 128)
    return pltpu.make_async_copy(w_hbm.at[:, pl.ds(start, WINDOW)], place, sem)


def twice(x):
    return x.astype(BF16), jnp.concatenate([x[:, WINDOW - 64 :], x[:, : WINDOW - 64]], axis=1).astype(BF16)


def head_operands(head, core, q_ref, blocks):
    offset = head * HEAD_DIM + core * 64
    turned = (head + core) % 2
    inside = offset + 64 * turned
    start = pl.multiple_of(inside // 128 * 128, 128)
    inside = inside - start
    lane = lax.broadcasted_iota(jnp.int32, (1, 128), 1)
    mine = (lane >= inside) & (lane < inside + HEAD_DIM)
    queries = jnp.where(mine, q_ref[turned, :, pl.ds(start, 128)], jnp.zeros((), BF16))
    keys, values = [], []
    for k_ref, vt_ref in blocks:
        keys.append(k_ref[turned, :, pl.ds(start, 128)])
        first = lax.broadcasted_iota(jnp.int32, (AUG - HEAD_DIM, vt_ref.shape[1]), 0) == 0
        vt = vt_ref[pl.ds(pl.multiple_of(offset, 8), HEAD_DIM), :]
        values.append(jnp.concatenate([vt, jnp.where(first, 1.0, 0.0)], axis=0).astype(BF16))
    return queries, keys, values


def attend_heads(heads, halves, core, q_ref, blocks, old, known_top):
    operands = [head_operands(head, core, q_ref, blocks) for head in heads]
    items = [(i, half) for i in range(len(heads)) for half in halves]

    def score(item):
        i, half = item
        queries, keys, _ = operands[i]
        part = queries[half * ROWS : (half + 1) * ROWS]
        return [lax.dot_general(k, part, NT, preferred_element_type=F32) for k in keys]

    out = []
    ahead = [score(item) for item in items[:LOOK]]
    for n, (i, half) in enumerate(items):
        scores = ahead.pop(0)
        if n + LOOK < len(items):
            ahead.append(score(items[n + LOOK]))
        tops = [jnp.max(part, axis=0, keepdims=True) for part in scores]
        top = tops[0]
        for more in tops[1:]:
            top = jnp.maximum(top, more)
        total = None
        reference = top
        if old is not None:
            acc_ref, top_ref = old
            before = top_ref[half, heads[i], 0:1, :]
            total = acc_ref[half, heads[i]]
            if known_top:
                reference = before
            else:
                reference = jnp.maximum(top, before)
                total = total * jnp.exp2(before - reference)
        for value, part in zip(operands[i][2], scores):
            term = jnp.dot(value, jnp.exp2(part - reference).astype(BF16), preferred_element_type=F32)
            total = term if total is None else total + term
        out.append((total, reference, top))
    return out


def keys_values(xn, w_ref, k_ref, vt_ref):
    packed = jnp.dot(xn, w_ref[...], preferred_element_type=F32)
    k_ref[0], k_ref[1] = twice(packed[:, :WINDOW])
    vt_ref[...] = packed[:, WINDOW:].T


def near_kernel(
    core_ref, xo_hbm, xp_ref, mod_hbm, w_hbm, next_hbm, q_ref, acc_ref, top_ref, mod_ref, w_ref, next_ref, wq_ref, xo_ref, xn_ref, k_ref, vt_ref, sems
):
    core = core_ref[0]
    own = pltpu.make_async_copy(xo_hbm, xo_ref, sems.at[3])
    mod = pltpu.make_async_copy(mod_hbm, mod_ref, sems.at[4])
    mod.start()
    own.start()
    copies = [
        window_copy(w_hbm, 0, core, wq_ref, sems.at[0]),
        window_copy(w_hbm, 1, core, w_ref.at[:, :WINDOW], sems.at[1]),
        window_copy(w_hbm, 2, core, w_ref.at[:, WINDOW:], sems.at[2]),
    ]
    for copy in copies:
        copy.start()
    following = pltpu.make_async_copy(next_hbm, next_ref, sems.at[5])
    following.start()
    mod.wait()
    xn_ref[ROWS:, :] = modulate(xp_ref[...], mod_ref[0:1, :], mod_ref[1:2, :])
    own.wait()
    xn_ref[0:ROWS, :] = modulate(xo_ref[...], mod_ref[0:1, :], mod_ref[1:2, :])
    copies[0].wait()
    queries = jnp.dot(xn_ref[...], wq_ref[...], preferred_element_type=F32)
    q_ref[0], q_ref[1] = twice(queries * QSCALE)
    copies[1].wait()
    copies[2].wait()
    keys_values(xn_ref[...], w_ref, k_ref, vt_ref)


    def some(p, carry):
        heads = [2 * p + i for i in range(2)]
        results = attend_heads(heads, (0, 1), core, q_ref, ((k_ref, vt_ref),), None, False)
        for n, (total, top, _) in enumerate(results):
            acc_ref[n % 2, heads[n // 2]] = total
            top_ref[n % 2, heads[n // 2]] = jnp.broadcast_to(top, (8, ROWS))
        return carry

    lax.fori_loop(0, 8 // 2, some, 0)
    following.wait()


def near(core, xo, xp, mod, w, following):
    return pl.pallas_call(
        near_kernel,
        in_specs=[SMEM, HBM, VMEM, HBM, HBM, HBM],
        out_specs=[VMEM] * 6,
        out_shape=[
            jax.ShapeDtypeStruct((2, QUERIES, WINDOW), BF16),
            jax.ShapeDtypeStruct((2, 8, AUG, ROWS), F32),
            jax.ShapeDtypeStruct((2, 8, 8, ROWS), F32),
            jax.ShapeDtypeStruct((6, WIDTH), F32),
            jax.ShapeDtypeStruct((WIDTH, 2 * WINDOW), BF16),
            jax.ShapeDtypeStruct((WIDTH, 3 * WIDTH), BF16),
        ],
        scratch_shapes=[
            pltpu.VMEM((WIDTH, WINDOW), BF16),
            pltpu.VMEM((ROWS, WIDTH), BF16),
            pltpu.VMEM((QUERIES, WIDTH), BF16),
            pltpu.VMEM((2, QUERIES, WINDOW), BF16),
            pltpu.VMEM((WINDOW, QUERIES), F32),
            pltpu.SemaphoreType.DMA((6,)),
        ],
        compiler_params=params(36),
        cost_estimate=pl.CostEstimate(flops=1_000_000, bytes_accessed=100_000, transcendentals=0),
        name="near_tokens",
    )(core, xo, xp, mod, w, following)


def project_kernel(x_ref, mod_ref, w_ref, k_ref, vt_ref):
    xn = modulate(x_ref[...], mod_ref[0:1, :], mod_ref[1:2, :])
    keys_values(xn, w_ref, k_ref, vt_ref)


def project(x, mod, w):
    return pl.pallas_call(
        project_kernel,
        in_specs=[VMEM] * 3,
        out_specs=[VMEM] * 2,
        out_shape=[jax.ShapeDtypeStruct((2, ROWS, WINDOW), BF16), jax.ShapeDtypeStruct((WINDOW, ROWS), F32)],
        compiler_params=params(14),
        cost_estimate=pl.CostEstimate(flops=1_000_000, bytes_accessed=100_000, transcendentals=0),
        name="far_keys",
    )(x, mod, w)


def attend_far(half, core, q_ref, blocks, acc_ref, top_ref, out_ref, over_ref):
    def attend(first, count, known_top):
        heads = [first + i for i in range(count)]
        done = []
        for total, reference, top in attend_heads(heads, (half,), core, q_ref, blocks, (acc_ref, top_ref), known_top):
            if known_top:
                over_ref[0:1, :] = jnp.maximum(over_ref[0:1, :], top - reference)
            done.append(total[:HEAD_DIM] / total[HEAD_DIM : HEAD_DIM + 1])
        for i in range(0, count, 2):
            rows = pl.ds(pl.multiple_of((first + i) * HEAD_DIM, 16), 2 * HEAD_DIM)
            out_ref[rows, :ROWS] = jnp.concatenate(done[i : i + 2], axis=0).astype(BF16)

    over_ref[...] = jnp.zeros_like(over_ref)
    attend(0, 8, True)

    @pl.when(jnp.max(over_ref[...]) > EXCESS)
    def _():
        def pair(p, carry):
            attend(2 * p, 2, False)
            return carry

        lax.fori_loop(0, 4, pair, 0)


def far_peer_kernel(
    core_ref, x_ref, mod_ref, w_ref, k1_ref, vt1_ref, q_ref, acc_ref, top_ref, out_ref, k_ref, vt_ref, over_ref
):
    xn = modulate(x_ref[...], mod_ref[0:1, :], mod_ref[1:2, :])
    keys_values(xn, w_ref, k_ref, vt_ref)
    out_ref[:, ROWS:] = jnp.zeros((HALF_COLS, PADDED - ROWS), BF16)
    blocks = ((k1_ref, vt1_ref), (k_ref, vt_ref))
    attend_far(1, core_ref[0], q_ref, blocks, acc_ref, top_ref, out_ref, over_ref)


def far_peer(core, x, mod, w, k1, vt1, q, acc, top):
    return pl.pallas_call(
        far_peer_kernel,
        in_specs=[SMEM] + [VMEM] * 8,
        out_specs=[VMEM] * 3,
        out_shape=[
            jax.ShapeDtypeStruct((HALF_COLS, PADDED), BF16),
            jax.ShapeDtypeStruct((2, ROWS, WINDOW), BF16),
            jax.ShapeDtypeStruct((WINDOW, ROWS), F32),
        ],
        scratch_shapes=[pltpu.VMEM((8, ROWS), F32)],
        compiler_params=params(28),
        cost_estimate=pl.CostEstimate(flops=10_000_000_000, bytes_accessed=10_000_000, transcendentals=3_200_000),
        name="far_peer_queries",
    )(core, x, mod, w, k1, vt1, q, acc, top)


def far_own_kernel(core_ref, k1_ref, vt1_ref, k2_ref, vt2_ref, q_ref, acc_ref, top_ref, out_ref, over_ref):
    blocks = ((k1_ref, vt1_ref), (k2_ref, vt2_ref))
    attend_far(0, core_ref[0], q_ref, blocks, acc_ref, top_ref, out_ref, over_ref)


def far_own(core, k1, vt1, k2, vt2, q, acc, top):
    return pl.pallas_call(
        far_own_kernel,
        in_specs=[SMEM] + [VMEM] * 7,
        out_specs=VMEM,
        out_shape=jax.ShapeDtypeStruct((HALF_COLS, ROWS), BF16),
        scratch_shapes=[pltpu.VMEM((8, ROWS), F32)],
        compiler_params=params(24),
        cost_estimate=pl.CostEstimate(flops=8_000_000_000, bytes_accessed=5_000_000, transcendentals=3_200_000),
        name="far_own_queries",
    )(core, k1, vt1, k2, vt2, q, acc, top)


def join_kernel(core_ref, mine_ref, other_ref, x_ref, mod_ref, wo_ref, out_ref, att_ref):
    core = core_ref[0]
    att_ref[pl.ds(pl.multiple_of(core * HALF_COLS, 16), HALF_COLS), :] = mine_ref[...]
    att_ref[pl.ds(pl.multiple_of((1 - core) * HALF_COLS, 16), HALF_COLS), :] = other_ref[:, :ROWS]
    projected = lax.dot_general(att_ref[...], wo_ref[...], TN, preferred_element_type=F32)
    middle = x_ref[...].astype(F32) + mod_ref[2:3, :] * projected
    for d in range(16):
        for i in range(7):
            out_ref[d, i] = middle[28 * d + 4 * i : 28 * d + 4 * i + 4].astype(BF16)


def join(core, mine, other, x, mod, wo):
    return pl.pallas_call(
        join_kernel,
        in_specs=[SMEM] + [VMEM] * 5,
        out_specs=VMEM,
        out_shape=jax.ShapeDtypeStruct((16, 7, 4, WIDTH), BF16),
        scratch_shapes=[pltpu.VMEM((WIDTH, ROWS), BF16)],
        compiler_params=params(14),
        cost_estimate=pl.CostEstimate(flops=1_200_000_000, bytes_accessed=6_000_000, transcendentals=0),
        name="spatial_out",
    )(core, mine, other, x, mod, wo)


def temporal_kernel(mid_ref, mod_ref, w_ref, wo_ref, out_ref, x_ref, q_ref, k_ref, vt_ref, att_ref):
    for f in range(16):
        for i in range(7):
            at = ((i // 2 * 16) + f) * 8 + i % 2 * 4 if i < 6 else 384 + 4 * f
            x_ref[at : at + 4, :] = mid_ref[f, i].astype(F32)
    xn = modulate(x_ref[...], mod_ref[3:4, :], mod_ref[4:5, :])
    packed = jnp.dot(xn, w_ref[...], preferred_element_type=F32)
    q_ref[:, ROWS:] = jnp.zeros((WIDTH, PADDED - ROWS), BF16)
    q_ref[:, :ROWS] = (packed[:, :WIDTH] * QSCALE).T.astype(BF16)
    k_ref[...] = packed[:, WIDTH : 2 * WIDTH].astype(BF16)
    vt_ref[...] = packed[:, 2 * WIDTH :].T

    row = lax.broadcasted_iota(jnp.int32, (256, 1), 0)
    none = jnp.zeros((), BF16)

    def rows_of(g):
        return slice(g * 128, min(g * 128 + 128, ROWS))

    def score(g, p):
        queries = q_ref[128 * p : 128 * p + 256, g * 128 : g * 128 + 128]
        inside = 16 * p
        first = jnp.where((row >= inside) & (row < inside + HEAD_DIM), queries, none)
        second = jnp.where((row >= inside + HEAD_DIM) & (row < inside + 2 * HEAD_DIM), queries, none)
        keys = k_ref[rows_of(g), 128 * p : 128 * p + 256]
        return jnp.dot(keys, jnp.concatenate([first, second], axis=1), preferred_element_type=F32)

    def weigh(g, scores):
        every = 8 if g < 3 else 4
        shape = scores.shape
        key_token = lax.broadcasted_iota(jnp.int32, shape, 0) % every
        same = key_token == lax.broadcasted_iota(jnp.int32, shape, 1) % every
        scores = jnp.where(same, scores, -1e30)
        top = jnp.max(scores, axis=0, keepdims=True)
        return jnp.exp2(scores - top).astype(BF16)

    def value(g, p, weights):
        at = 2 * HEAD_DIM * p
        tail = jnp.where(lax.broadcasted_iota(jnp.int32, (AUG - HEAD_DIM, weights.shape[0]), 0) == 0, 1.0, 0.0)
        first = vt_ref[at : at + HEAD_DIM, rows_of(g)]
        second = vt_ref[at + HEAD_DIM : at + 2 * HEAD_DIM, rows_of(g)]
        values = jnp.concatenate([first, tail, second, tail], axis=0).astype(BF16)
        return jnp.dot(values, weights, preferred_element_type=F32)

    def finish(g, p, total):
        at = 2 * HEAD_DIM * p
        first = total[:HEAD_DIM, :128] / total[HEAD_DIM : HEAD_DIM + 1, :128]
        second = total[AUG : AUG + HEAD_DIM, 128:] / total[AUG + HEAD_DIM : AUG + HEAD_DIM + 1, 128:]
        both = jnp.concatenate([first, second], axis=0).astype(BF16)
        att_ref[at : at + 2 * HEAD_DIM, g * 128 : g * 128 + 128] = both

    order = [(g, p) for g in range(4) for p in range(8)]
    apart = 4
    scores, totals = {}, {}
    for i in range(len(order) + 2 * apart):
        if i < len(order):
            scores[i] = score(*order[i])
        j = i - apart
        if 0 <= j < len(order):
            g, p = order[j]
            totals[j] = value(g, p, weigh(g, scores.pop(j)))
        k = i - 2 * apart
        if 0 <= k < len(order):
            finish(*order[k], totals.pop(k))

    projected = lax.dot_general(att_ref[:, :ROWS], wo_ref[...], TN, preferred_element_type=F32)
    x_ref[...] = x_ref[...] + mod_ref[5:6, :] * projected
    for f in range(16):
        for i in range(7):
            at = ((i // 2 * 16) + f) * 8 + i % 2 * 4 if i < 6 else 384 + 4 * f
            out_ref[f, i] = x_ref[at : at + 4, :].astype(BF16)


def temporal(mid, mod, w, wo):
    return pl.pallas_call(
        temporal_kernel,
        in_specs=[VMEM] * 4,
        out_specs=VMEM,
        out_shape=jax.ShapeDtypeStruct((16, 7, 4, WIDTH), BF16),
        scratch_shapes=[
            pltpu.VMEM((ROWS, WIDTH), F32),
            pltpu.VMEM((WIDTH, PADDED), BF16),
            pltpu.VMEM((ROWS, WIDTH), BF16),
            pltpu.VMEM((WIDTH, ROWS), F32),
            pltpu.VMEM((WIDTH, PADDED), BF16),
        ],
        compiler_params=params(24),
        cost_estimate=pl.CostEstimate(flops=6_000_000_000, bytes_accessed=14_000_000, transcendentals=1_000_000),
        name="temporal_block",
    )(mid, mod, w, wo)


def local(clip, modulation, w_qkv_s, w_out_s, w_qkv_t, w_out_t):
    own = clip[0]
    core = (lax.axis_index("head") % 2).astype(jnp.int32).reshape(1)
    swap_chip = [(0, 2), (1, 3), (2, 0), (3, 1)]
    swap_core = [(0, 1), (1, 0), (2, 3), (3, 2)]
    peer = lax.ppermute(own, "head", swap_core)
    there = lax.ppermute(own, "head", swap_chip)
    q, acc, top, mod, w, w_t = near(core, own, peer, modulation, w_qkv_s, w_qkv_t)
    there, q = lax.optimization_barrier((there, q))
    k1, vt1 = project(there, mod, w)
    there_peer = lax.ppermute(there, "head", swap_core)
    theirs, k2, vt2 = far_peer(core, there_peer, mod, w, k1, vt1, q, acc, top)
    other = lax.ppermute(theirs, "head", swap_core)
    mine = far_own(core, k1, vt1, k2, vt2, q, acc, top)
    middle = join(core, mine, other, own, mod, w_out_s)
    block = lax.all_to_all(middle, "tm", split_axis=0, concat_axis=0, tiled=True)
    done = temporal(block, modulation, w_t, w_out_t)
    back = lax.all_to_all(done, "tm", split_axis=0, concat_axis=0, tiled=True)
    return back.reshape(1, ROWS, WIDTH)


def solution(mesh):
    placed = (P(("dp", "tm"), "head", None), P("dp", None), P(), P(), P(), P())
    return jax.shard_map(
        local, mesh=mesh, in_specs=placed, out_specs=P(("dp", "tm"), "head", None), check_vma=False
    )
```

profile of v0, /device:TPU:0, one launch (start us, length us, event | category | flops | bytes accessed | tf_op | source)
XLA Modules:
  0.0 96.0 jit_solution(3170930102181524674)
XLA Ops:
  0.0 0.0 collective-permute-start.1
  0.0 3.1 %collective-permute-start = (bf16[448,1152]{1,0:T(8,128)(2,1)}, bf16[448,1152]{1,0:T(8,128)(2,1)S(1)}, u32[]{:S(2)}, u32[]{:S(2)}) collective-permute-start(bf16[448,1152]{1,0:T(8,128)(2,1)} %bitcast.3), channel_id=1, source_target_pairs={{0,2},{1,3},{2,0},{3,1},{4,6},{5,7},{6,4},{7,5},{8,10},{9,11},{10,... | collective-permute-start | bytes 3096584 | tf_op jit(solution)/shard_map/ppermute | solution.py:390
  3.1 0.0 collective-permute-done.1.xp_ref
  3.1 0.0 copy-start
  3.1 1.2 %copy-done = bf16[1,448,1152]{2,1,0:T(8,128)(2,1)S(1)} copy-done((bf16[1,448,1152]{2,1,0:T(8,128)(2,1)S(1)}, bf16[1,448,1152]{2,1,0:T(8,128)(2,1)}, u32[]{:S(2)}) %copy-start) | copy-done | bytes 1032216
  4.4 0.0 copy-start.3
  4.4 0.8 copy-done.3
  5.1 17.5 %near_tokens.1 = (bf16[2,896,640]{2,1,0:T(8,128)(2,1)S(1)}, f32[2,8,80,448]{3,2,1,0:T(8,128)S(1)}, f32[2,8,8,448]{3,2,1,0:T(8,128)S(1)}, f32[6,1152]{1,0:T(8,128...) custom-call(s32[1]{0:T(128)} %bitcast.core_ref, bf16[448,1152]{1,0:T(8,128)(2,1)S(1)} %bitcast.4, ...), custom_call_target="tpu_custom_call" | custom-call | flops 1000000 | bytes 100000 | tf_op jit(solution)/shard_map/near_tokens/pallas_call | solution.py:157
  22.6 4.3 %collective-permute-done.x_ref = bf16[448,1152]{1,0:T(8,128)(2,1)S(1)} collective-permute-done((bf16[448,1152]{1,0:T(8,128)(2,1)}, bf16[448,1152]{1,0:T(8,128)(2,1)S(1)}, u32[]{:S(2)}, u32[]{:S(2)}) %collective-permute-start) | collective-permute-done | bytes 1032224 | tf_op jit(solution)/shard_map/ppermute | solution.py:390
  26.9 0.0 collective-permute-start.2
  26.9 2.4 %far_keys.1 = (bf16[2,448,640]{2,1,0:T(8,128)(2,1)S(1)}, f32[640,448]{1,0:T(8,128)S(1)}) custom-call(bf16[448,1152]{1,0:T(8,128)(2,1)S(1)} %collective-permute-done.x_ref, f32[6,1152]{1,0:T(8,128)S(1)} %get-tuple-element.20.mod_ref, bf16[1152,1280]{1,0:T(8,128)(2,1)S(1)} %get-tuple-element.21.w_ref), custom_call_target="tpu_custom_call" | custom-call | flops 1000000 | bytes 100000 | tf_op jit(solution)/shard_map/far_keys/pallas_call | solution.py:189
  29.3 0.2 collective-permute-done.2.x_ref
  29.6 5.7 %far_peer_queries.1 = (bf16[576,512]{1,0:T(8,128)(2,1)S(1)}, bf16[2,448,640]{2,1,0:T(8,128)(2,1)S(1)}, f32[640,448]{1,0:T(8,128)S(1)}) custom-call(s32[1]{0:T(128)} %bitcast.core_ref, bf16[448,1152]{1,0:T(8,128)(2,1)S(1)} %collective-permute-done.2.x_ref, f32[6,1152]{1,0:T(8,128)S(1)} %get-tuple-element.20.mod_ref, ...), custom_call_target="tpu_custom_call" | custom-call | flops 10000000000 | bytes 10000000 | tf_op jit(solution)/shard_map/far_peer_queries/pallas_call | solution.py:235
  35.2 0.4 collective-permute-start.3
  35.6 0.0 copy-start.1
  35.6 0.0 copy-start.2
  35.6 3.9 %far_own_queries.1.mine_ref = bf16[576,448]{1,0:T(8,128)(2,1)S(1)} custom-call(s32[1]{0:T(128)} %bitcast.core_ref, bf16[2,448,640]{2,1,0:T(8,128)(2,1)S(1)} %get-tuple-element.22.k1_ref, f32[640,448]{1,0:T(8,128)S(1)} %get-tuple-element.23.vt1_ref, bf16[2,448,640]{2,1,0:T(8,128)(2,1)S(1)} %get-tuple-element.27.k2_ref, ...), custom_call_target="tpu_custom_call" | custom-call | flops 8000000000 | bytes 5000000 | tf_op jit(solution)/shard_map/far_own_queries/pallas_call | solution.py:257
  39.5 0.0 copy-start.4
  39.5 0.0 copy-start.5
  39.5 0.0 collective-permute-done.3.other_ref
  39.5 0.0 copy-done.1
  39.5 0.0 copy-done.2
  39.5 1.8 %spatial_out.1 = bf16[16,7,4,1152]{3,2,1,0:T(4,128)(2,1)S(1)} custom-call(s32[1]{0:T(128)} %bitcast.core_ref, bf16[576,448]{1,0:T(8,128)(2,1)S(1)} %far_own_queries.1.mine_ref, bf16[576,512]{1,0:T(8,128)(2,1)S(1)} %collective-permute-done.3.other_ref, bf16[448,1152]{1,0:T(8,128)(2,1)S(1)} %bitcast.5, f32[6,1152]{1,0:T(8,128)S(1)} %get-tuple-element.20.mod_ref, ...), custom_call_target="tpu_custom_call" | custom-call | flops 1200000000 | bytes 6000000 | tf_op jit(solution)/shard_map/spatial_out/pallas_call | solution.py:281
  41.4 25.3 %all_to_all.10.mid_ref = bf16[16,7,4,1152]{3,2,1,0:T(4,128)(2,1)S(1)} all-to-all(bf16[16,7,4,1152]{3,2,1,0:T(4,128)(2,1)S(1)} %spatial_out.1), channel_id=1, replica_groups=mesh['dp'=2,'tm'=16,'head'=4] {'tm'}, dimensions={0} | all-to-all | bytes 2064384 | tf_op jit(solution)/shard_map/all_to_all | solution.py:399
  66.7 0.0 copy-done.4
  66.7 0.0 copy-done.5
  66.7 8.7 %temporal_block.1 = bf16[16,7,4,1152]{3,2,1,0:T(4,128)(2,1)S(1)} custom-call(bf16[16,7,4,1152]{3,2,1,0:T(4,128)(2,1)S(1)} %all_to_all.10.mid_ref, f32[6,1152]{1,0:T(8,128)S(1)} %copy-done.4, bf16[1152,3456]{1,0:T(8,128)(2,1)S(1)} %get-tuple-element.30.w_ref, bf16[1152,1152]{1,0:T(8,128)(2,1)S(1)} %copy-done.5), custom_call_target="tpu_custom_call" | custom-call | flops 6000000000 | bytes 14000000 | tf_op jit(solution)/shard_map/temporal_block/pallas_call | solution.py:366
  75.4 19.4 %all_to_all.11 = bf16[16,7,4,1152]{3,2,1,0:T(4,128)(2,1)S(1)} all-to-all(bf16[16,7,4,1152]{3,2,1,0:T(4,128)(2,1)S(1)} %temporal_block.1), channel_id=1, replica_groups=mesh['dp'=2,'tm'=16,'head'=4] {'tm'}, dimensions={0} | all-to-all | bytes 2064384 | tf_op jit(solution)/shard_map/all_to_all | solution.py:401
  94.8 1.2 %reshape.7 = bf16[1,448,1152]{2,1,0:T(8,128)(2,1)} reshape(bf16[16,7,4,1152]{3,2,1,0:T(4,128)(2,1)S(1)} %all_to_all.11) | data formatting | bytes 2064384 | tf_op jit(solution)/shard_map/reshape | solution.py:402
Async XLA Ops:
  0.0 3.1 %collective-permute-start.1 = (bf16[448,1152]{1,0:T(8,128)(2,1)}, bf16[448,1152]{1,0:T(8,128)(2,1)S(1)}, u32[]{:S(2)}, u32[]{:S(2)}) collective-permute-start(bf16[448,1152]{1,0:T(8,128)(2,1)} %bitcast.2), channel_id=1, source_target_pairs={{0,1},{1,0},{2,3},{3,2},{4,5},{5,4},{6,7},{7,6},{8,9},{9,8},{10,11... | collective-permute-start | bytes 3096584 | tf_op jit(solution)/shard_map/ppermute | solution.py:389
  0.0 26.9 %collective-permute-start = (bf16[448,1152]{1,0:T(8,128)(2,1)}, bf16[448,1152]{1,0:T(8,128)(2,1)S(1)}, u32[]{:S(2)}, u32[]{:S(2)}) collective-permute-start(bf16[448,1152]{1,0:T(8,128)(2,1)} %bitcast.3), channel_id=1, source_target_pairs={{0,2},{1,3},{2,0},{3,1},{4,6},{5,7},{6,4},{7,5},{8,10},{9,11},{10,... | collective-permute-start | bytes 3096584 | tf_op jit(solution)/shard_map/ppermute | solution.py:390
  3.1 1.2 %copy-start = (bf16[1,448,1152]{2,1,0:T(8,128)(2,1)S(1)}, bf16[1,448,1152]{2,1,0:T(8,128)(2,1)}, u32[]{:S(2)}) copy-start(bf16[1,448,1152]{2,1,0:T(8,128)(2,1)} %param.6) | copy-start | bytes 3096580
  4.4 0.8 copy-start.3
  26.9 2.6 %collective-permute-start.2 = (bf16[448,1152]{1,0:T(8,128)(2,1)S(1)}, bf16[448,1152]{1,0:T(8,128)(2,1)S(1)}, u32[]{:S(2)}, u32[]{:S(2)}) collective-permute-start(bf16[448,1152]{1,0:T(8,128)(2,1)S(1)} %collective-permute-done.x_ref), channel_id=1, source_target_pairs={{0,1},{1,0},{2,3},{3,2},{4,5},{5,4},{6,7},{7,6},{8,9},{9,8},{10,11... | collective-permute-start | bytes 3096584 | tf_op jit(solution)/shard_map/ppermute | solution.py:394
  35.2 4.3 %collective-permute-start.3 = (bf16[576,512]{1,0:T(8,128)(2,1)S(1)}, bf16[576,512]{1,0:T(8,128)(2,1)S(1)}, u32[]{:S(2)}, u32[]{:S(2)}) collective-permute-start(bf16[576,512]{1,0:T(8,128)(2,1)S(1)} %get-tuple-element.29), channel_id=1, source_target_pairs={{0,1},{1,0},{2,3},{3,2},{4,5},{5,4},{6,7},{7,6},{8,9},{9,8},{10,11... | collective-permute-start | bytes 1769480 | tf_op jit(solution)/shard_map/ppermute | solution.py:396
  35.6 3.9 %copy-start.1 = (bf16[1,448,1152]{2,1,0:T(8,128)(2,1)S(1)}, bf16[1,448,1152]{2,1,0:T(8,128)(2,1)}, u32[]{:S(2)}) copy-start(bf16[1,448,1152]{2,1,0:T(8,128)(2,1)} %param.6) | copy-start | bytes 3096580
  35.6 3.9 %copy-start.2 = (bf16[1152,1152]{1,0:T(8,128)(2,1)S(1)}, bf16[1152,1152]{1,0:T(8,128)(2,1)}, u32[]{:S(2)}) copy-start(bf16[1152,1152]{1,0:T(8,128)(2,1)} %wo_ref.2) | copy-start | bytes 7962628
  39.5 27.2 %copy-start.4 = (f32[6,1152]{1,0:T(8,128)S(1)}, f32[6,1152]{1,0:T(8,128)}, u32[]{:S(2)}) copy-start(f32[6,1152]{1,0:T(8,128)} %mod_ref.1) | copy-start | bytes 82948
  39.5 27.2 %copy-start.5 = (bf16[1152,1152]{1,0:T(8,128)(2,1)S(1)}, bf16[1152,1152]{1,0:T(8,128)(2,1)}, u32[]{:S(2)}) copy-start(bf16[1152,1152]{1,0:T(8,128)(2,1)} %wo_ref.3) | copy-start | bytes 7962628
where the time goes:
time: 96.3 us; the launch traced here: 96 us
  blocking collectives  44.7 us (46%)
  Pallas kernels  39.9 us (41%)
  waiting for transfers between devices  4.54 us (5%)
  starting transfers between devices  3.48 us (4%)
  local copies, waits for them, and re-layouts  3.23 us (3%)
    all_to_all x1, blocking collectives, local(): lax.all_to_all(middle, 'tm', split_axis=0, concat_axis=0, tiled=True)  25.3 us
    all_to_all x1, blocking collectives, local(): back = lax.all_to_all(done, 'tm', split_axis=0, concat_axis=0, tiled=True)  19.4 us
    pallas_call x1, Pallas kernels, near(): pl.pallas_call(near_kernel, in_specs=[SMEM, HBM, VMEM, HBM, HBM, HBM], ou...  17.5 us
    pallas_call x1, Pallas kernels, temporal(): pl.pallas_call(temporal_kernel, in_specs=[VMEM] * 4, out_specs=VMEM, out_...  8.68 us
    pallas_call x1, Pallas kernels, far_peer(): pl.pallas_call(far_peer_kernel, in_specs=[SMEM] + [VMEM] * 8, out_specs=[...  5.66 us
    ppermute x1, waiting for transfers between devices, local(): there = lax.ppermute(own, 'head', swap_chip)  4.29 us
    pallas_call x1, Pallas kernels, far_own(): pl.pallas_call(far_own_kernel, in_specs=[SMEM] + [VMEM] * 7, out_specs=VM...  3.87 us
    ppermute x1, starting transfers between devices, local(): there = lax.ppermute(own, 'head', swap_chip)  3.11 us
  transfers between devices with their start and end apart: 4, of which 2 were waited for; matrix products, arithmetic and copies ran while one was open for 0% of the time, Pallas kernels for 25%

commit v1 on v0

--- a/solution.py
+++ b/solution.py
@@ -266,12 +266,13 @@
     )(core, k1, vt1, k2, vt2, q, acc, top)
 
 
-def join_kernel(core_ref, mine_ref, other_ref, x_ref, mod_ref, wo_ref, out_ref, att_ref):
+def join_kernel(core_ref, mine_ref, other_ref, x_ref, mod_ref, wo_ref, out_ref, kept_ref, att_ref):
     core = core_ref[0]
     att_ref[pl.ds(pl.multiple_of(core * HALF_COLS, 16), HALF_COLS), :] = mine_ref[...]
     att_ref[pl.ds(pl.multiple_of((1 - core) * HALF_COLS, 16), HALF_COLS), :] = other_ref[:, :ROWS]
     projected = lax.dot_general(att_ref[...], wo_ref[...], TN, preferred_element_type=F32)
     middle = x_ref[...].astype(F32) + mod_ref[2:3, :] * projected
+    kept_ref[...] = middle.astype(BF16)
     for d in range(16):
         for i in range(7):
             out_ref[d, i] = middle[28 * d + 4 * i : 28 * d + 4 * i + 4].astype(BF16)
@@ -281,8 +282,8 @@
     return pl.pallas_call(
         join_kernel,
         in_specs=[SMEM] + [VMEM] * 5,
-        out_specs=VMEM,
-        out_shape=jax.ShapeDtypeStruct((16, 7, 4, WIDTH), BF16),
+        out_specs=[VMEM] * 2,
+        out_shape=[jax.ShapeDtypeStruct((16, 7, 4, WIDTH), BF16), jax.ShapeDtypeStruct((ROWS, WIDTH), BF16)],
         scratch_shapes=[pltpu.VMEM((WIDTH, ROWS), BF16)],
         compiler_params=params(14),
         cost_estimate=pl.CostEstimate(flops=1_200_000_000, bytes_accessed=6_000_000, transcendentals=0),
@@ -290,7 +291,7 @@
     )(core, mine, other, x, mod, wo)
 
 
-def temporal_kernel(mid_ref, mod_ref, w_ref, wo_ref, out_ref, x_ref, q_ref, k_ref, vt_ref, att_ref):
+def temporal_kernel(mid_ref, mod_ref, w_ref, out_ref, x_ref, q_ref, k_ref, vt_ref, att_ref):
     for f in range(16):
         for i in range(7):
             at = ((i // 2 * 16) + f) * 8 + i % 2 * 4 if i < 6 else 384 + 4 * f
@@ -337,8 +338,17 @@
         at = 2 * HEAD_DIM * p
         first = total[:HEAD_DIM, :128] / total[HEAD_DIM : HEAD_DIM + 1, :128]
         second = total[AUG : AUG + HEAD_DIM, 128:] / total[AUG + HEAD_DIM : AUG + HEAD_DIM + 1, 128:]
-        both = jnp.concatenate([first, second], axis=0).astype(BF16)
-        att_ref[at : at + 2 * HEAD_DIM, g * 128 : g * 128 + 128] = both
+        att_ref[at : at + HEAD_DIM, g * 128 : g * 128 + 128] = first
+        att_ref[at + HEAD_DIM : at + 2 * HEAD_DIM, g * 128 : g * 128 + 128] = second
+
+    def send(g):
+        rows = att_ref[:, g * 128 : g * 128 + 128].T
+        for f in range(16):
+            if g == 3:
+                out_ref[f, 6] = rows[4 * f : 4 * f + 4].astype(BF16)
+            else:
+                out_ref[f, 2 * g] = rows[8 * f : 8 * f + 4].astype(BF16)
+                out_ref[f, 2 * g + 1] = rows[8 * f + 4 : 8 * f + 8].astype(BF16)
 
     order = [(g, p) for g in range(4) for p in range(8)]
     apart = 4
@@ -353,19 +363,14 @@
         k = i - 2 * apart
         if 0 <= k < len(order):
             finish(*order[k], totals.pop(k))
-
-    projected = lax.dot_general(att_ref[:, :ROWS], wo_ref[...], TN, preferred_element_type=F32)
-    x_ref[...] = x_ref[...] + mod_ref[5:6, :] * projected
-    for f in range(16):
-        for i in range(7):
-            at = ((i // 2 * 16) + f) * 8 + i % 2 * 4 if i < 6 else 384 + 4 * f
-            out_ref[f, i] = x_ref[at : at + 4, :].astype(BF16)
-
-
-def temporal(mid, mod, w, wo):
+            if order[k][1] == 7:
+                send(order[k][0])
+
+
+def temporal(mid, mod, w):
     return pl.pallas_call(
         temporal_kernel,
-        in_specs=[VMEM] * 4,
+        in_specs=[VMEM] * 3,
         out_specs=VMEM,
         out_shape=jax.ShapeDtypeStruct((16, 7, 4, WIDTH), BF16),
         scratch_shapes=[
@@ -373,12 +378,35 @@
             pltpu.VMEM((WIDTH, PADDED), BF16),
             pltpu.VMEM((ROWS, WIDTH), BF16),
             pltpu.VMEM((WIDTH, ROWS), F32),
-            pltpu.VMEM((WIDTH, PADDED), BF16),
+            pltpu.VMEM((WIDTH, PADDED), F32),
         ],
-        compiler_params=params(24),
-        cost_estimate=pl.CostEstimate(flops=6_000_000_000, bytes_accessed=14_000_000, transcendentals=1_000_000),
-        name="temporal_block",
-    )(mid, mod, w, wo)
+        compiler_params=params(26),
+        cost_estimate=pl.CostEstimate(flops=5_000_000_000, bytes_accessed=10_000_000, transcendentals=1_000_000),
+        name="temporal_attention",
+    )(mid, mod, w)
+
+
+def last_kernel(att_ref, mid_ref, mod_ref, wo_ref, out_ref, rows_ref):
+    for part in range(2):
+        rows = slice(part * ROWS // 2, (part + 1) * ROWS // 2)
+        for d in range(8 * part, 8 * part + 8):
+            for i in range(7):
+                rows_ref[28 * d + 4 * i : 28 * d + 4 * i + 4, :] = att_ref[d, i].astype(F32)
+        projected = jnp.dot(rows_ref[rows, :].astype(BF16), wo_ref[...], preferred_element_type=F32)
+        out_ref[rows, :] = (mid_ref[rows, :].astype(F32) + mod_ref[5:6, :] * projected).astype(BF16)
+
+
+def last(att, mid, mod, wo):
+    return pl.pallas_call(
+        last_kernel,
+        in_specs=[VMEM] * 4,
+        out_specs=VMEM,
+        out_shape=jax.ShapeDtypeStruct((ROWS, WIDTH), BF16),
+        scratch_shapes=[pltpu.VMEM((ROWS, WIDTH), F32)],
+        compiler_params=params(14),
+        cost_estimate=pl.CostEstimate(flops=1_200_000_000, bytes_accessed=6_000_000, transcendentals=0),
+        name="temporal_out",
+    )(att, mid, mod, wo)
 
 
 def local(clip, modulation, w_qkv_s, w_out_s, w_qkv_t, w_out_t):
@@ -395,11 +423,11 @@
     theirs, k2, vt2 = far_peer(core, there_peer, mod, w, k1, vt1, q, acc, top)
     other = lax.ppermute(theirs, "head", swap_core)
     mine = far_own(core, k1, vt1, k2, vt2, q, acc, top)
-    middle = join(core, mine, other, own, mod, w_out_s)
+    middle, kept = join(core, mine, other, own, mod, w_out_s)
     block = lax.all_to_all(middle, "tm", split_axis=0, concat_axis=0, tiled=True)
-    done = temporal(block, modulation, w_t, w_out_t)
-    back = lax.all_to_all(done, "tm", split_axis=0, concat_axis=0, tiled=True)
-    return back.reshape(1, ROWS, WIDTH)
+    attended = temporal(block, mod, w_t)
+    back = lax.all_to_all(attended, "tm", split_axis=0, concat_axis=0, tiled=True)
+    return last(back, kept, mod, w_out_t).reshape(1, ROWS, WIDTH)
 
 
 def solution(mesh):

time: 96.3 us -> 95.8 us (level)
  local copies, waits for them, and re-layouts: 3.23 us -> 2.03 us
    reshape x1 -> x0, local copies, waits for them, and re-layouts: 1.2 us -> none  [local(): return back.reshape(1, ROWS, WIDTH)]
    pallas_call x2 -> x3, Pallas kernels: 10.5 us -> 11.3 us  [the longest x1 6.76 us: temporal(): pl.pallas_call(temporal_kernel, in_specs=[VMEM] * 3, out_specs=VMEM, out_...]
    unnamed x12 -> x10, local copies, waits for them, and re-layouts: 2.04 us -> 2.03 us
where the time goes in v1:
time: 95.8 us; the launch traced here: 95.5 us
  blocking collectives  44.7 us (47%)
  Pallas kernels  40.7 us (42%)
  waiting for transfers between devices  4.54 us (5%)
  starting transfers between devices  3.48 us (4%)
  local copies, waits for them, and re-layouts  2.03 us (2%)
    all_to_all x1, blocking collectives, local(): lax.all_to_all(middle, 'tm', split_axis=0, concat_axis=0, tiled=True)  25.3 us
    all_to_all x1, blocking collectives, local(): lax.all_to_all(attended, 'tm', split_axis=0, concat_axis=0, tiled=True)  19.4 us
    pallas_call x1, Pallas kernels, near(): pl.pallas_call(near_kernel, in_specs=[SMEM, HBM, VMEM, HBM, HBM, HBM], ou...  17.5 us
    pallas_call x1, Pallas kernels, temporal(): pl.pallas_call(temporal_kernel, in_specs=[VMEM] * 3, out_specs=VMEM, out_...  6.76 us
    pallas_call x1, Pallas kernels, far_peer(): pl.pallas_call(far_peer_kernel, in_specs=[SMEM] + [VMEM] * 8, out_specs=[...  5.66 us
    ppermute x1, waiting for transfers between devices, local(): there = lax.ppermute(own, 'head', swap_chip)  4.29 us
    pallas_call x1, Pallas kernels, far_own(): pl.pallas_call(far_own_kernel, in_specs=[SMEM] + [VMEM] * 7, out_specs=VM...  3.87 us
    ppermute x1, starting transfers between devices, local(): there = lax.ppermute(own, 'head', swap_chip)  3.11 us
  transfers between devices with their start and end apart: 4, of which 2 were waited for; matrix products, arithmetic and copies ran while one was open for 0% of the time, Pallas kernels for 25%

profile of v1, /device:TPU:0, one launch (start us, length us, event | category | flops | bytes accessed | tf_op | source)
XLA Modules:
  0.0 95.5 jit_solution(15311550986975998868)
XLA Ops:
  0.0 0.0 collective-permute-start.1
  0.0 3.1 %collective-permute-start = (bf16[448,1152]{1,0:T(8,128)(2,1)}, bf16[448,1152]{1,0:T(8,128)(2,1)S(1)}, u32[]{:S(2)}, u32[]{:S(2)}) collective-permute-start(bf16[448,1152]{1,0:T(8,128)(2,1)} %bitcast.4), channel_id=1, source_target_pairs={{0,2},{1,3},{2,0},{3,1},{4,6},{5,7},{6,4},{7,5},{8,10},{9,11},{10,... | collective-permute-start | bytes 3096584 | tf_op jit(solution)/shard_map/ppermute | solution.py:418
  3.1 0.0 collective-permute-done.1.xp_ref
  3.1 0.0 copy-start
  3.1 1.2 %copy-done = bf16[1,448,1152]{2,1,0:T(8,128)(2,1)S(1)} copy-done((bf16[1,448,1152]{2,1,0:T(8,128)(2,1)S(1)}, bf16[1,448,1152]{2,1,0:T(8,128)(2,1)}, u32[]{:S(2)}) %copy-start) | copy-done | bytes 1032216
  4.4 0.0 copy-start.4
  4.4 0.8 copy-done.4
  5.1 17.5 %near_tokens.1 = (bf16[2,896,640]{2,1,0:T(8,128)(2,1)S(1)}, f32[2,8,80,448]{3,2,1,0:T(8,128)S(1)}, f32[2,8,8,448]{3,2,1,0:T(8,128)S(1)}, f32[6,1152]{1,0:T(8,128...) custom-call(s32[1]{0:T(128)} %bitcast.core_ref, bf16[448,1152]{1,0:T(8,128)(2,1)S(1)} %bitcast.5, ...), custom_call_target="tpu_custom_call" | custom-call | flops 1000000 | bytes 100000 | tf_op jit(solution)/shard_map/near_tokens/pallas_call | solution.py:157
  22.6 4.3 %collective-permute-done.x_ref = bf16[448,1152]{1,0:T(8,128)(2,1)S(1)} collective-permute-done((bf16[448,1152]{1,0:T(8,128)(2,1)}, bf16[448,1152]{1,0:T(8,128)(2,1)S(1)}, u32[]{:S(2)}, u32[]{:S(2)}) %collective-permute-start) | collective-permute-done | bytes 1032224 | tf_op jit(solution)/shard_map/ppermute | solution.py:418
  26.9 0.0 collective-permute-start.2
  26.9 2.4 %far_keys.1 = (bf16[2,448,640]{2,1,0:T(8,128)(2,1)S(1)}, f32[640,448]{1,0:T(8,128)S(1)}) custom-call(bf16[448,1152]{1,0:T(8,128)(2,1)S(1)} %collective-permute-done.x_ref, f32[6,1152]{1,0:T(8,128)S(1)} %get-tuple-element.22.mod_ref, bf16[1152,1280]{1,0:T(8,128)(2,1)S(1)} %get-tuple-element.23.w_ref), custom_call_target="tpu_custom_call" | custom-call | flops 1000000 | bytes 100000 | tf_op jit(solution)/shard_map/far_keys/pallas_call | solution.py:189
  29.3 0.2 collective-permute-done.2.x_ref
  29.6 5.7 %far_peer_queries.1 = (bf16[576,512]{1,0:T(8,128)(2,1)S(1)}, bf16[2,448,640]{2,1,0:T(8,128)(2,1)S(1)}, f32[640,448]{1,0:T(8,128)S(1)}) custom-call(s32[1]{0:T(128)} %bitcast.core_ref, bf16[448,1152]{1,0:T(8,128)(2,1)S(1)} %collective-permute-done.2.x_ref, f32[6,1152]{1,0:T(8,128)S(1)} %get-tuple-element.22.mod_ref, ...), custom_call_target="tpu_custom_call" | custom-call | flops 10000000000 | bytes 10000000 | tf_op jit(solution)/shard_map/far_peer_queries/pallas_call | solution.py:235
  35.2 0.4 collective-permute-start.3
  35.6 0.0 copy-start.1
  35.6 0.0 copy-start.3
  35.6 3.9 %far_own_queries.1.mine_ref = bf16[576,448]{1,0:T(8,128)(2,1)S(1)} custom-call(s32[1]{0:T(128)} %bitcast.core_ref, bf16[2,448,640]{2,1,0:T(8,128)(2,1)S(1)} %get-tuple-element.24.k1_ref, f32[640,448]{1,0:T(8,128)S(1)} %get-tuple-element.25.vt1_ref, bf16[2,448,640]{2,1,0:T(8,128)(2,1)S(1)} %get-tuple-element.29.k2_ref, ...), custom_call_target="tpu_custom_call" | custom-call | flops 8000000000 | bytes 5000000 | tf_op jit(solution)/shard_map/far_own_queries/pallas_call | solution.py:257
  39.5 0.0 collective-permute-done.3.other_ref
  39.5 0.0 copy-done.1
  39.5 0.0 copy-done.3
  39.5 1.8 %spatial_out.1 = (bf16[16,7,4,1152]{3,2,1,0:T(4,128)(2,1)S(1)}, bf16[448,1152]{1,0:T(8,128)(2,1)S(1)}) custom-call(s32[1]{0:T(128)} %bitcast.core_ref, bf16[576,448]{1,0:T(8,128)(2,1)S(1)} %far_own_queries.1.mine_ref, bf16[576,512]{1,0:T(8,128)(2,1)S(1)} %collective-permute-done.3.other_ref, bf16[448,1152]{1,0:T(8,128)(2,1)S(1)} %bitcast.6, ...), custom_call_target="tpu_custom_call" | custom-call | flops 1200000000 | bytes 6000000 | tf_op jit(solution)/shard_map/spatial_out/pallas_call | solution.py:282
  41.4 25.3 %all_to_all.10.mid_ref = bf16[16,7,4,1152]{3,2,1,0:T(4,128)(2,1)S(1)} all-to-all(bf16[16,7,4,1152]{3,2,1,0:T(4,128)(2,1)S(1)} %get-tuple-element.32), channel_id=1, replica_groups=mesh['dp'=2,'tm'=16,'head'=4] {'tm'}, dimensions={0} | all-to-all | bytes 2064384 | tf_op jit(solution)/shard_map/all_to_all | solution.py:427
  66.7 0.0 copy-start.2
  66.7 6.8 %temporal_attention.1 = bf16[16,7,4,1152]{3,2,1,0:T(4,128)(2,1)S(1)} custom-call(bf16[16,7,4,1152]{3,2,1,0:T(4,128)(2,1)S(1)} %all_to_all.10.mid_ref, f32[6,1152]{1,0:T(8,128)S(1)} %get-tuple-element.22.mod_ref, bf16[1152,3456]{1,0:T(8,128)(2,1)S(1)} %get-tuple-element.33.w_ref), custom_call_target="tpu_custom_call" | custom-call | flops 5000000000 | bytes 10000000 | tf_op jit(solution)/shard_map/temporal_attention/pallas_call | solution.py:371
  73.4 19.4 %all_to_all.11.att_ref = bf16[16,7,4,1152]{3,2,1,0:T(4,128)(2,1)S(1)} all-to-all(bf16[16,7,4,1152]{3,2,1,0:T(4,128)(2,1)S(1)} %temporal_attention.1), channel_id=1, replica_groups=mesh['dp'=2,'tm'=16,'head'=4] {'tm'}, dimensions={0} | all-to-all | bytes 2064384 | tf_op jit(solution)/shard_map/all_to_all | solution.py:429
  92.9 0.0 copy-done.2
  92.9 2.7 %temporal_out.1 = bf16[448,1152]{1,0:T(8,128)(2,1)} custom-call(bf16[16,7,4,1152]{3,2,1,0:T(4,128)(2,1)S(1)} %all_to_all.11.att_ref, bf16[448,1152]{1,0:T(8,128)(2,1)S(1)} %get-tuple-element.34.mid_ref, f32[6,1152]{1,0:T(8,128)S(1)} %get-tuple-element.22.mod_ref, bf16[1152,1152]{1,0:T(8,128)(2,1)S(1)} %copy-done.2), custom_call_target="tpu_custom_call" | custom-call | flops 1200000000 | bytes 6000000 | tf_op jit(solution)/shard_map/temporal_out/pallas_call | solution.py:400
Async XLA Ops:
  0.0 3.1 %collective-permute-start.1 = (bf16[448,1152]{1,0:T(8,128)(2,1)}, bf16[448,1152]{1,0:T(8,128)(2,1)S(1)}, u32[]{:S(2)}, u32[]{:S(2)}) collective-permute-start(bf16[448,1152]{1,0:T(8,128)(2,1)} %bitcast.3), channel_id=1, source_target_pairs={{0,1},{1,0},{2,3},{3,2},{4,5},{5,4},{6,7},{7,6},{8,9},{9,8},{10,11... | collective-permute-start | bytes 3096584 | tf_op jit(solution)/shard_map/ppermute | solution.py:417
  0.0 26.9 %collective-permute-start = (bf16[448,1152]{1,0:T(8,128)(2,1)}, bf16[448,1152]{1,0:T(8,128)(2,1)S(1)}, u32[]{:S(2)}, u32[]{:S(2)}) collective-permute-start(bf16[448,1152]{1,0:T(8,128)(2,1)} %bitcast.4), channel_id=1, source_target_pairs={{0,2},{1,3},{2,0},{3,1},{4,6},{5,7},{6,4},{7,5},{8,10},{9,11},{10,... | collective-permute-start | bytes 3096584 | tf_op jit(solution)/shard_map/ppermute | solution.py:418
  3.1 1.2 %copy-start = (bf16[1,448,1152]{2,1,0:T(8,128)(2,1)S(1)}, bf16[1,448,1152]{2,1,0:T(8,128)(2,1)}, u32[]{:S(2)}) copy-start(bf16[1,448,1152]{2,1,0:T(8,128)(2,1)} %param.6) | copy-start | bytes 3096580
  4.4 0.8 copy-start.4
  26.9 2.6 %collective-permute-start.2 = (bf16[448,1152]{1,0:T(8,128)(2,1)S(1)}, bf16[448,1152]{1,0:T(8,128)(2,1)S(1)}, u32[]{:S(2)}, u32[]{:S(2)}) collective-permute-start(bf16[448,1152]{1,0:T(8,128)(2,1)S(1)} %collective-permute-done.x_ref), channel_id=1, source_target_pairs={{0,1},{1,0},{2,3},{3,2},{4,5},{5,4},{6,7},{7,6},{8,9},{9,8},{10,11... | collective-permute-start | bytes 3096584 | tf_op jit(solution)/shard_map/ppermute | solution.py:422
  35.2 4.2 %collective-permute-start.3 = (bf16[576,512]{1,0:T(8,128)(2,1)S(1)}, bf16[576,512]{1,0:T(8,128)(2,1)S(1)}, u32[]{:S(2)}, u32[]{:S(2)}) collective-permute-start(bf16[576,512]{1,0:T(8,128)(2,1)S(1)} %get-tuple-element.31), channel_id=1, source_target_pairs={{0,1},{1,0},{2,3},{3,2},{4,5},{5,4},{6,7},{7,6},{8,9},{9,8},{10,11... | collective-permute-start | bytes 1769480 | tf_op jit(solution)/shard_map/ppermute | solution.py:424
  35.6 3.9 %copy-start.1 = (bf16[1,448,1152]{2,1,0:T(8,128)(2,1)S(1)}, bf16[1,448,1152]{2,1,0:T(8,128)(2,1)}, u32[]{:S(2)}) copy-start(bf16[1,448,1152]{2,1,0:T(8,128)(2,1)} %param.6) | copy-start | bytes 3096580
  35.6 3.9 %copy-start.3 = (bf16[1152,1152]{1,0:T(8,128)(2,1)S(1)}, bf16[1152,1152]{1,0:T(8,128)(2,1)}, u32[]{:S(2)}) copy-start(bf16[1152,1152]{1,0:T(8,128)(2,1)} %wo_ref.2) | copy-start | bytes 7962628
  66.7 26.2 %copy-start.2 = (bf16[1152,1152]{1,0:T(8,128)(2,1)S(1)}, bf16[1152,1152]{1,0:T(8,128)(2,1)}, u32[]{:S(2)}) copy-start(bf16[1152,1152]{1,0:T(8,128)(2,1)} %wo_ref.3) | copy-start | bytes 7962628

commit v2 on v1

--- a/solution.py
+++ b/solution.py
@@ -16,7 +16,7 @@
 HALF_COLS = 576
 AUG = 80
 PADDED = 512
-LOOK = 2
+LOOK = 4
 QSCALE = math.log2(math.e) / math.sqrt(HEAD_DIM)
 NT = (((1,), (1,)), ((), ()))
 TN = (((0,), (0,)), ((), ()))
@@ -351,7 +351,7 @@
                 out_ref[f, 2 * g + 1] = rows[8 * f + 4 : 8 * f + 8].astype(BF16)
 
     order = [(g, p) for g in range(4) for p in range(8)]
-    apart = 4
+    apart = 8
     scores, totals = {}, {}
     for i in range(len(order) + 2 * apart):
         if i < len(order):

time: 95.8 us -> 95.7 us (level)
  no operation moved by 1% of the time
where the time goes in v2:
time: 95.7 us; the launch traced here: 95.4 us
  blocking collectives  44.7 us (47%)
  Pallas kernels  40.7 us (43%)
  waiting for transfers between devices  4.36 us (5%)
  starting transfers between devices  3.49 us (4%)
  local copies, waits for them, and re-layouts  2.03 us (2%)
    all_to_all x1, blocking collectives, local(): lax.all_to_all(middle, 'tm', split_axis=0, concat_axis=0, tiled=True)  25.3 us
    all_to_all x1, blocking collectives, local(): lax.all_to_all(attended, 'tm', split_axis=0, concat_axis=0, tiled=True)  19.4 us
    pallas_call x1, Pallas kernels, near(): pl.pallas_call(near_kernel, in_specs=[SMEM, HBM, VMEM, HBM, HBM, HBM], ou...  17.7 us
    pallas_call x1, Pallas kernels, temporal(): pl.pallas_call(temporal_kernel, in_specs=[VMEM] * 3, out_specs=VMEM, out_...  6.71 us
    pallas_call x1, Pallas kernels, far_peer(): pl.pallas_call(far_peer_kernel, in_specs=[SMEM] + [VMEM] * 8, out_specs=[...  5.63 us
    ppermute x1, waiting for transfers between devices, local(): there = lax.ppermute(own, 'head', swap_chip)  4.12 us
    pallas_call x1, Pallas kernels, far_own(): pl.pallas_call(far_own_kernel, in_specs=[SMEM] + [VMEM] * 7, out_specs=VM...  3.81 us
    ppermute x1, starting transfers between devices, local(): there = lax.ppermute(own, 'head', swap_chip)  3.11 us
  transfers between devices with their start and end apart: 4, of which 2 were waited for; matrix products, arithmetic and copies ran while one was open for 0% of the time, Pallas kernels for 25%

profile of v2, /device:TPU:0, one launch (start us, length us, event | category | flops | bytes accessed | tf_op | source)
XLA Modules:
  0.0 95.4 jit_solution(3711773249307514964)
XLA Ops:
  0.0 0.0 collective-permute-start.1
  0.0 3.1 %collective-permute-start = (bf16[448,1152]{1,0:T(8,128)(2,1)}, bf16[448,1152]{1,0:T(8,128)(2,1)S(1)}, u32[]{:S(2)}, u32[]{:S(2)}) collective-permute-start(bf16[448,1152]{1,0:T(8,128)(2,1)} %bitcast.4), channel_id=1, source_target_pairs={{0,2},{1,3},{2,0},{3,1},{4,6},{5,7},{6,4},{7,5},{8,10},{9,11},{10,... | collective-permute-start | bytes 3096584 | tf_op jit(solution)/shard_map/ppermute | solution.py:418
  3.1 0.0 collective-permute-done.1.xp_ref
  3.1 0.0 copy-start
  3.1 1.2 %copy-done = bf16[1,448,1152]{2,1,0:T(8,128)(2,1)S(1)} copy-done((bf16[1,448,1152]{2,1,0:T(8,128)(2,1)S(1)}, bf16[1,448,1152]{2,1,0:T(8,128)(2,1)}, u32[]{:S(2)}) %copy-start) | copy-done | bytes 1032216
  4.4 0.0 copy-start.4
  4.4 0.8 copy-done.4
  5.1 17.7 %near_tokens.1 = (bf16[2,896,640]{2,1,0:T(8,128)(2,1)S(1)}, f32[2,8,80,448]{3,2,1,0:T(8,128)S(1)}, f32[2,8,8,448]{3,2,1,0:T(8,128)S(1)}, f32[6,1152]{1,0:T(8,128...) custom-call(s32[1]{0:T(128)} %bitcast.core_ref, bf16[448,1152]{1,0:T(8,128)(2,1)S(1)} %bitcast.5, ...), custom_call_target="tpu_custom_call" | custom-call | flops 1000000 | bytes 100000 | tf_op jit(solution)/shard_map/near_tokens/pallas_call | solution.py:157
  22.8 4.1 %collective-permute-done.x_ref = bf16[448,1152]{1,0:T(8,128)(2,1)S(1)} collective-permute-done((bf16[448,1152]{1,0:T(8,128)(2,1)}, bf16[448,1152]{1,0:T(8,128)(2,1)S(1)}, u32[]{:S(2)}, u32[]{:S(2)}) %collective-permute-start) | collective-permute-done | bytes 1032224 | tf_op jit(solution)/shard_map/ppermute | solution.py:418
  26.9 0.0 collective-permute-start.2
  26.9 2.4 %far_keys.1 = (bf16[2,448,640]{2,1,0:T(8,128)(2,1)S(1)}, f32[640,448]{1,0:T(8,128)S(1)}) custom-call(bf16[448,1152]{1,0:T(8,128)(2,1)S(1)} %collective-permute-done.x_ref, f32[6,1152]{1,0:T(8,128)S(1)} %get-tuple-element.22.mod_ref, bf16[1152,1280]{1,0:T(8,128)(2,1)S(1)} %get-tuple-element.23.w_ref), custom_call_target="tpu_custom_call" | custom-call | flops 1000000 | bytes 100000 | tf_op jit(solution)/shard_map/far_keys/pallas_call | solution.py:189
  29.3 0.2 collective-permute-done.2.x_ref
  29.6 5.6 %far_peer_queries.1 = (bf16[576,512]{1,0:T(8,128)(2,1)S(1)}, bf16[2,448,640]{2,1,0:T(8,128)(2,1)S(1)}, f32[640,448]{1,0:T(8,128)S(1)}) custom-call(s32[1]{0:T(128)} %bitcast.core_ref, bf16[448,1152]{1,0:T(8,128)(2,1)S(1)} %collective-permute-done.2.x_ref, f32[6,1152]{1,0:T(8,128)S(1)} %get-tuple-element.22.mod_ref, ...), custom_call_target="tpu_custom_call" | custom-call | flops 10000000000 | bytes 10000000 | tf_op jit(solution)/shard_map/far_peer_queries/pallas_call | solution.py:235
  35.2 0.4 collective-permute-start.3
  35.6 0.0 copy-start.1
  35.6 0.0 copy-start.3
  35.6 3.8 %far_own_queries.1.mine_ref = bf16[576,448]{1,0:T(8,128)(2,1)S(1)} custom-call(s32[1]{0:T(128)} %bitcast.core_ref, bf16[2,448,640]{2,1,0:T(8,128)(2,1)S(1)} %get-tuple-element.24.k1_ref, f32[640,448]{1,0:T(8,128)S(1)} %get-tuple-element.25.vt1_ref, bf16[2,448,640]{2,1,0:T(8,128)(2,1)S(1)} %get-tuple-element.29.k2_ref, ...), custom_call_target="tpu_custom_call" | custom-call | flops 8000000000 | bytes 5000000 | tf_op jit(solution)/shard_map/far_own_queries/pallas_call | solution.py:257
  39.4 0.0 collective-permute-done.3.other_ref
  39.4 0.0 copy-done.1
  39.4 0.0 copy-done.3
  39.4 1.8 %spatial_out.1 = (bf16[16,7,4,1152]{3,2,1,0:T(4,128)(2,1)S(1)}, bf16[448,1152]{1,0:T(8,128)(2,1)S(1)}) custom-call(s32[1]{0:T(128)} %bitcast.core_ref, bf16[576,448]{1,0:T(8,128)(2,1)S(1)} %far_own_queries.1.mine_ref, bf16[576,512]{1,0:T(8,128)(2,1)S(1)} %collective-permute-done.3.other_ref, bf16[448,1152]{1,0:T(8,128)(2,1)S(1)} %bitcast.6, ...), custom_call_target="tpu_custom_call" | custom-call | flops 1200000000 | bytes 6000000 | tf_op jit(solution)/shard_map/spatial_out/pallas_call | solution.py:282
  41.3 25.3 %all_to_all.10.mid_ref = bf16[16,7,4,1152]{3,2,1,0:T(4,128)(2,1)S(1)} all-to-all(bf16[16,7,4,1152]{3,2,1,0:T(4,128)(2,1)S(1)} %get-tuple-element.32), channel_id=1, replica_groups=mesh['dp'=2,'tm'=16,'head'=4] {'tm'}, dimensions={0} | all-to-all | bytes 2064384 | tf_op jit(solution)/shard_map/all_to_all | solution.py:427
  66.6 0.0 copy-start.2
  66.6 6.7 %temporal_attention.1 = bf16[16,7,4,1152]{3,2,1,0:T(4,128)(2,1)S(1)} custom-call(bf16[16,7,4,1152]{3,2,1,0:T(4,128)(2,1)S(1)} %all_to_all.10.mid_ref, f32[6,1152]{1,0:T(8,128)S(1)} %get-tuple-element.22.mod_ref, bf16[1152,3456]{1,0:T(8,128)(2,1)S(1)} %get-tuple-element.33.w_ref), custom_call_target="tpu_custom_call" | custom-call | flops 5000000000 | bytes 10000000 | tf_op jit(solution)/shard_map/temporal_attention/pallas_call | solution.py:371
  73.3 19.4 %all_to_all.11.att_ref = bf16[16,7,4,1152]{3,2,1,0:T(4,128)(2,1)S(1)} all-to-all(bf16[16,7,4,1152]{3,2,1,0:T(4,128)(2,1)S(1)} %temporal_attention.1), channel_id=1, replica_groups=mesh['dp'=2,'tm'=16,'head'=4] {'tm'}, dimensions={0} | all-to-all | bytes 2064384 | tf_op jit(solution)/shard_map/all_to_all | solution.py:429
  92.7 0.0 copy-done.2
  92.7 2.7 %temporal_out.1 = bf16[448,1152]{1,0:T(8,128)(2,1)} custom-call(bf16[16,7,4,1152]{3,2,1,0:T(4,128)(2,1)S(1)} %all_to_all.11.att_ref, bf16[448,1152]{1,0:T(8,128)(2,1)S(1)} %get-tuple-element.34.mid_ref, f32[6,1152]{1,0:T(8,128)S(1)} %get-tuple-element.22.mod_ref, bf16[1152,1152]{1,0:T(8,128)(2,1)S(1)} %copy-done.2), custom_call_target="tpu_custom_call" | custom-call | flops 1200000000 | bytes 6000000 | tf_op jit(solution)/shard_map/temporal_out/pallas_call | solution.py:400
Async XLA Ops:
  0.0 3.1 %collective-permute-start.1 = (bf16[448,1152]{1,0:T(8,128)(2,1)}, bf16[448,1152]{1,0:T(8,128)(2,1)S(1)}, u32[]{:S(2)}, u32[]{:S(2)}) collective-permute-start(bf16[448,1152]{1,0:T(8,128)(2,1)} %bitcast.3), channel_id=1, source_target_pairs={{0,1},{1,0},{2,3},{3,2},{4,5},{5,4},{6,7},{7,6},{8,9},{9,8},{10,11... | collective-permute-start | bytes 3096584 | tf_op jit(solution)/shard_map/ppermute | solution.py:417
  0.0 26.9 %collective-permute-start = (bf16[448,1152]{1,0:T(8,128)(2,1)}, bf16[448,1152]{1,0:T(8,128)(2,1)S(1)}, u32[]{:S(2)}, u32[]{:S(2)}) collective-permute-start(bf16[448,1152]{1,0:T(8,128)(2,1)} %bitcast.4), channel_id=1, source_target_pairs={{0,2},{1,3},{2,0},{3,1},{4,6},{5,7},{6,4},{7,5},{8,10},{9,11},{10,... | collective-permute-start | bytes 3096584 | tf_op jit(solution)/shard_map/ppermute | solution.py:418
  3.1 1.2 %copy-start = (bf16[1,448,1152]{2,1,0:T(8,128)(2,1)S(1)}, bf16[1,448,1152]{2,1,0:T(8,128)(2,1)}, u32[]{:S(2)}) copy-start(bf16[1,448,1152]{2,1,0:T(8,128)(2,1)} %param.6) | copy-start | bytes 3096580
  4.4 0.8 copy-start.4
  26.9 2.6 %collective-permute-start.2 = (bf16[448,1152]{1,0:T(8,128)(2,1)S(1)}, bf16[448,1152]{1,0:T(8,128)(2,1)S(1)}, u32[]{:S(2)}, u32[]{:S(2)}) collective-permute-start(bf16[448,1152]{1,0:T(8,128)(2,1)S(1)} %collective-permute-done.x_ref), channel_id=1, source_target_pairs={{0,1},{1,0},{2,3},{3,2},{4,5},{5,4},{6,7},{7,6},{8,9},{9,8},{10,11... | collective-permute-start | bytes 3096584 | tf_op jit(solution)/shard_map/ppermute | solution.py:422
  35.2 4.2 %collective-permute-start.3 = (bf16[576,512]{1,0:T(8,128)(2,1)S(1)}, bf16[576,512]{1,0:T(8,128)(2,1)S(1)}, u32[]{:S(2)}, u32[]{:S(2)}) collective-permute-start(bf16[576,512]{1,0:T(8,128)(2,1)S(1)} %get-tuple-element.31), channel_id=1, source_target_pairs={{0,1},{1,0},{2,3},{3,2},{4,5},{5,4},{6,7},{7,6},{8,9},{9,8},{10,11... | collective-permute-start | bytes 1769480 | tf_op jit(solution)/shard_map/ppermute | solution.py:424
  35.6 3.8 %copy-start.1 = (bf16[1,448,1152]{2,1,0:T(8,128)(2,1)S(1)}, bf16[1,448,1152]{2,1,0:T(8,128)(2,1)}, u32[]{:S(2)}) copy-start(bf16[1,448,1152]{2,1,0:T(8,128)(2,1)} %param.6) | copy-start | bytes 3096580
  35.6 3.8 %copy-start.3 = (bf16[1152,1152]{1,0:T(8,128)(2,1)S(1)}, bf16[1152,1152]{1,0:T(8,128)(2,1)}, u32[]{:S(2)}) copy-start(bf16[1152,1152]{1,0:T(8,128)(2,1)} %wo_ref.2) | copy-start | bytes 7962628
  66.6 26.1 %copy-start.2 = (bf16[1152,1152]{1,0:T(8,128)(2,1)S(1)}, bf16[1152,1152]{1,0:T(8,128)(2,1)}, u32[]{:S(2)}) copy-start(bf16[1152,1152]{1,0:T(8,128)(2,1)} %wo_ref.3) | copy-start | bytes 7962628

commit v3 on v1

--- a/solution.py
+++ b/solution.py
@@ -204,7 +204,7 @@
         for total, reference, top in attend_heads(heads, (half,), core, q_ref, blocks, (acc_ref, top_ref), known_top):
             if known_top:
                 over_ref[0:1, :] = jnp.maximum(over_ref[0:1, :], top - reference)
-            done.append(total[:HEAD_DIM] / total[HEAD_DIM : HEAD_DIM + 1])
+            done.append(total[:HEAD_DIM] * (1.0 / total[HEAD_DIM : HEAD_DIM + 1]))
         for i in range(0, count, 2):
             rows = pl.ds(pl.multiple_of((first + i) * HEAD_DIM, 16), 2 * HEAD_DIM)
             out_ref[rows, :ROWS] = jnp.concatenate(done[i : i + 2], axis=0).astype(BF16)
@@ -336,8 +336,8 @@
 
     def finish(g, p, total):
         at = 2 * HEAD_DIM * p
-        first = total[:HEAD_DIM, :128] / total[HEAD_DIM : HEAD_DIM + 1, :128]
-        second = total[AUG : AUG + HEAD_DIM, 128:] / total[AUG + HEAD_DIM : AUG + HEAD_DIM + 1, 128:]
+        first = total[:HEAD_DIM, :128] * (1.0 / total[HEAD_DIM : HEAD_DIM + 1, :128])
+        second = total[AUG : AUG + HEAD_DIM, 128:] * (1.0 / total[AUG + HEAD_DIM : AUG + HEAD_DIM + 1, 128:])
         att_ref[at : at + HEAD_DIM, g * 128 : g * 128 + 128] = first
         att_ref[at + HEAD_DIM : at + 2 * HEAD_DIM, g * 128 : g * 128 + 128] = second
 

time: 95.8 us -> 95.8 us (level)
  no operation moved by 1% of the time
where the time goes in v3:
time: 95.8 us; the launch traced here: 95.5 us
  blocking collectives  44.8 us (47%)
  Pallas kernels  40.7 us (42%)
  waiting for transfers between devices  4.54 us (5%)
  starting transfers between devices  3.46 us (4%)
  local copies, waits for them, and re-layouts  2.03 us (2%)
    all_to_all x1, blocking collectives, local(): lax.all_to_all(middle, 'tm', split_axis=0, concat_axis=0, tiled=True)  25.3 us
    all_to_all x1, blocking collectives, local(): lax.all_to_all(attended, 'tm', split_axis=0, concat_axis=0, tiled=True)  19.4 us
    pallas_call x1, Pallas kernels, near(): pl.pallas_call(near_kernel, in_specs=[SMEM, HBM, VMEM, HBM, HBM, HBM], ou...  17.5 us
    pallas_call x1, Pallas kernels, temporal(): pl.pallas_call(temporal_kernel, in_specs=[VMEM] * 3, out_specs=VMEM, out_...  6.77 us
    pallas_call x1, Pallas kernels, far_peer(): pl.pallas_call(far_peer_kernel, in_specs=[SMEM] + [VMEM] * 8, out_specs=[...  5.65 us
    ppermute x1, waiting for transfers between devices, local(): there = lax.ppermute(own, 'head', swap_chip)  4.29 us
    pallas_call x1, Pallas kernels, far_own(): pl.pallas_call(far_own_kernel, in_specs=[SMEM] + [VMEM] * 7, out_specs=VM...  3.84 us
    ppermute x1, starting transfers between devices, local(): there = lax.ppermute(own, 'head', swap_chip)  3.11 us
  transfers between devices with their start and end apart: 4, of which 2 were waited for; matrix products, arithmetic and copies ran while one was open for 0% of the time, Pallas kernels for 25%

profile of v3, /device:TPU:0, one launch (start us, length us, event | category | flops | bytes accessed | tf_op | source)
XLA Modules:
  0.0 95.5 jit_solution(16781186285231751267)
XLA Ops:
  0.0 0.0 collective-permute-start.1
  0.0 3.1 %collective-permute-start = (bf16[448,1152]{1,0:T(8,128)(2,1)}, bf16[448,1152]{1,0:T(8,128)(2,1)S(1)}, u32[]{:S(2)}, u32[]{:S(2)}) collective-permute-start(bf16[448,1152]{1,0:T(8,128)(2,1)} %bitcast.4), channel_id=1, source_target_pairs={{0,2},{1,3},{2,0},{3,1},{4,6},{5,7},{6,4},{7,5},{8,10},{9,11},{10,... | collective-permute-start | bytes 3096584 | tf_op jit(solution)/shard_map/ppermute | solution.py:418
  3.1 0.0 collective-permute-done.1.xp_ref
  3.1 0.0 copy-start
  3.1 1.2 %copy-done = bf16[1,448,1152]{2,1,0:T(8,128)(2,1)S(1)} copy-done((bf16[1,448,1152]{2,1,0:T(8,128)(2,1)S(1)}, bf16[1,448,1152]{2,1,0:T(8,128)(2,1)}, u32[]{:S(2)}) %copy-start) | copy-done | bytes 1032216
  4.4 0.0 copy-start.4
  4.4 0.8 copy-done.4
  5.1 17.5 %near_tokens.1 = (bf16[2,896,640]{2,1,0:T(8,128)(2,1)S(1)}, f32[2,8,80,448]{3,2,1,0:T(8,128)S(1)}, f32[2,8,8,448]{3,2,1,0:T(8,128)S(1)}, f32[6,1152]{1,0:T(8,128...) custom-call(s32[1]{0:T(128)} %bitcast.core_ref, bf16[448,1152]{1,0:T(8,128)(2,1)S(1)} %bitcast.5, ...), custom_call_target="tpu_custom_call" | custom-call | flops 1000000 | bytes 100000 | tf_op jit(solution)/shard_map/near_tokens/pallas_call | solution.py:157
  22.6 4.3 %collective-permute-done.x_ref = bf16[448,1152]{1,0:T(8,128)(2,1)S(1)} collective-permute-done((bf16[448,1152]{1,0:T(8,128)(2,1)}, bf16[448,1152]{1,0:T(8,128)(2,1)S(1)}, u32[]{:S(2)}, u32[]{:S(2)}) %collective-permute-start) | collective-permute-done | bytes 1032224 | tf_op jit(solution)/shard_map/ppermute | solution.py:418
  26.9 0.0 collective-permute-start.2
  26.9 2.4 %far_keys.1 = (bf16[2,448,640]{2,1,0:T(8,128)(2,1)S(1)}, f32[640,448]{1,0:T(8,128)S(1)}) custom-call(bf16[448,1152]{1,0:T(8,128)(2,1)S(1)} %collective-permute-done.x_ref, f32[6,1152]{1,0:T(8,128)S(1)} %get-tuple-element.22.mod_ref, bf16[1152,1280]{1,0:T(8,128)(2,1)S(1)} %get-tuple-element.23.w_ref), custom_call_target="tpu_custom_call" | custom-call | flops 1000000 | bytes 100000 | tf_op jit(solution)/shard_map/far_keys/pallas_call | solution.py:189
  29.3 0.2 collective-permute-done.2.x_ref
  29.6 5.7 %far_peer_queries.1 = (bf16[576,512]{1,0:T(8,128)(2,1)S(1)}, bf16[2,448,640]{2,1,0:T(8,128)(2,1)S(1)}, f32[640,448]{1,0:T(8,128)S(1)}) custom-call(s32[1]{0:T(128)} %bitcast.core_ref, bf16[448,1152]{1,0:T(8,128)(2,1)S(1)} %collective-permute-done.2.x_ref, f32[6,1152]{1,0:T(8,128)S(1)} %get-tuple-element.22.mod_ref, ...), custom_call_target="tpu_custom_call" | custom-call | flops 10000000000 | bytes 10000000 | tf_op jit(solution)/shard_map/far_peer_queries/pallas_call | solution.py:235
  35.2 0.3 collective-permute-start.3
  35.6 0.0 copy-start.1
  35.6 0.0 copy-start.3
  35.6 3.8 %far_own_queries.1.mine_ref = bf16[576,448]{1,0:T(8,128)(2,1)S(1)} custom-call(s32[1]{0:T(128)} %bitcast.core_ref, bf16[2,448,640]{2,1,0:T(8,128)(2,1)S(1)} %get-tuple-element.24.k1_ref, f32[640,448]{1,0:T(8,128)S(1)} %get-tuple-element.25.vt1_ref, bf16[2,448,640]{2,1,0:T(8,128)(2,1)S(1)} %get-tuple-element.29.k2_ref, ...), custom_call_target="tpu_custom_call" | custom-call | flops 8000000000 | bytes 5000000 | tf_op jit(solution)/shard_map/far_own_queries/pallas_call | solution.py:257
  39.4 0.0 collective-permute-done.3.other_ref
  39.5 0.0 copy-done.1
  39.5 0.0 copy-done.3
  39.5 1.8 %spatial_out.1 = (bf16[16,7,4,1152]{3,2,1,0:T(4,128)(2,1)S(1)}, bf16[448,1152]{1,0:T(8,128)(2,1)S(1)}) custom-call(s32[1]{0:T(128)} %bitcast.core_ref, bf16[576,448]{1,0:T(8,128)(2,1)S(1)} %far_own_queries.1.mine_ref, bf16[576,512]{1,0:T(8,128)(2,1)S(1)} %collective-permute-done.3.other_ref, bf16[448,1152]{1,0:T(8,128)(2,1)S(1)} %bitcast.6, ...), custom_call_target="tpu_custom_call" | custom-call | flops 1200000000 | bytes 6000000 | tf_op jit(solution)/shard_map/spatial_out/pallas_call | solution.py:282
  41.3 25.3 %all_to_all.10.mid_ref = bf16[16,7,4,1152]{3,2,1,0:T(4,128)(2,1)S(1)} all-to-all(bf16[16,7,4,1152]{3,2,1,0:T(4,128)(2,1)S(1)} %get-tuple-element.32), channel_id=1, replica_groups=mesh['dp'=2,'tm'=16,'head'=4] {'tm'}, dimensions={0} | all-to-all | bytes 2064384 | tf_op jit(solution)/shard_map/all_to_all | solution.py:427
  66.6 0.0 copy-start.2
  66.6 6.8 %temporal_attention.1 = bf16[16,7,4,1152]{3,2,1,0:T(4,128)(2,1)S(1)} custom-call(bf16[16,7,4,1152]{3,2,1,0:T(4,128)(2,1)S(1)} %all_to_all.10.mid_ref, f32[6,1152]{1,0:T(8,128)S(1)} %get-tuple-element.22.mod_ref, bf16[1152,3456]{1,0:T(8,128)(2,1)S(1)} %get-tuple-element.33.w_ref), custom_call_target="tpu_custom_call" | custom-call | flops 5000000000 | bytes 10000000 | tf_op jit(solution)/shard_map/temporal_attention/pallas_call | solution.py:371
  73.4 19.4 %all_to_all.11.att_ref = bf16[16,7,4,1152]{3,2,1,0:T(4,128)(2,1)S(1)} all-to-all(bf16[16,7,4,1152]{3,2,1,0:T(4,128)(2,1)S(1)} %temporal_attention.1), channel_id=1, replica_groups=mesh['dp'=2,'tm'=16,'head'=4] {'tm'}, dimensions={0} | all-to-all | bytes 2064384 | tf_op jit(solution)/shard_map/all_to_all | solution.py:429
  92.8 0.0 copy-done.2
  92.8 2.7 %temporal_out.1 = bf16[448,1152]{1,0:T(8,128)(2,1)} custom-call(bf16[16,7,4,1152]{3,2,1,0:T(4,128)(2,1)S(1)} %all_to_all.11.att_ref, bf16[448,1152]{1,0:T(8,128)(2,1)S(1)} %get-tuple-element.34.mid_ref, f32[6,1152]{1,0:T(8,128)S(1)} %get-tuple-element.22.mod_ref, bf16[1152,1152]{1,0:T(8,128)(2,1)S(1)} %copy-done.2), custom_call_target="tpu_custom_call" | custom-call | flops 1200000000 | bytes 6000000 | tf_op jit(solution)/shard_map/temporal_out/pallas_call | solution.py:400
Async XLA Ops:
  0.0 3.1 %collective-permute-start.1 = (bf16[448,1152]{1,0:T(8,128)(2,1)}, bf16[448,1152]{1,0:T(8,128)(2,1)S(1)}, u32[]{:S(2)}, u32[]{:S(2)}) collective-permute-start(bf16[448,1152]{1,0:T(8,128)(2,1)} %bitcast.3), channel_id=1, source_target_pairs={{0,1},{1,0},{2,3},{3,2},{4,5},{5,4},{6,7},{7,6},{8,9},{9,8},{10,11... | collective-permute-start | bytes 3096584 | tf_op jit(solution)/shard_map/ppermute | solution.py:417
  0.0 26.9 %collective-permute-start = (bf16[448,1152]{1,0:T(8,128)(2,1)}, bf16[448,1152]{1,0:T(8,128)(2,1)S(1)}, u32[]{:S(2)}, u32[]{:S(2)}) collective-permute-start(bf16[448,1152]{1,0:T(8,128)(2,1)} %bitcast.4), channel_id=1, source_target_pairs={{0,2},{1,3},{2,0},{3,1},{4,6},{5,7},{6,4},{7,5},{8,10},{9,11},{10,... | collective-permute-start | bytes 3096584 | tf_op jit(solution)/shard_map/ppermute | solution.py:418
  3.1 1.2 %copy-start = (bf16[1,448,1152]{2,1,0:T(8,128)(2,1)S(1)}, bf16[1,448,1152]{2,1,0:T(8,128)(2,1)}, u32[]{:S(2)}) copy-start(bf16[1,448,1152]{2,1,0:T(8,128)(2,1)} %param.6) | copy-start | bytes 3096580
  4.4 0.8 copy-start.4
  26.9 2.6 %collective-permute-start.2 = (bf16[448,1152]{1,0:T(8,128)(2,1)S(1)}, bf16[448,1152]{1,0:T(8,128)(2,1)S(1)}, u32[]{:S(2)}, u32[]{:S(2)}) collective-permute-start(bf16[448,1152]{1,0:T(8,128)(2,1)S(1)} %collective-permute-done.x_ref), channel_id=1, source_target_pairs={{0,1},{1,0},{2,3},{3,2},{4,5},{5,4},{6,7},{7,6},{8,9},{9,8},{10,11... | collective-permute-start | bytes 3096584 | tf_op jit(solution)/shard_map/ppermute | solution.py:422
  35.2 4.2 %collective-permute-start.3 = (bf16[576,512]{1,0:T(8,128)(2,1)S(1)}, bf16[576,512]{1,0:T(8,128)(2,1)S(1)}, u32[]{:S(2)}, u32[]{:S(2)}) collective-permute-start(bf16[576,512]{1,0:T(8,128)(2,1)S(1)} %get-tuple-element.31), channel_id=1, source_target_pairs={{0,1},{1,0},{2,3},{3,2},{4,5},{5,4},{6,7},{7,6},{8,9},{9,8},{10,11... | collective-permute-start | bytes 1769480 | tf_op jit(solution)/shard_map/ppermute | solution.py:424
  35.6 3.9 %copy-start.1 = (bf16[1,448,1152]{2,1,0:T(8,128)(2,1)S(1)}, bf16[1,448,1152]{2,1,0:T(8,128)(2,1)}, u32[]{:S(2)}) copy-start(bf16[1,448,1152]{2,1,0:T(8,128)(2,1)} %param.6) | copy-start | bytes 3096580
  35.6 3.9 %copy-start.3 = (bf16[1152,1152]{1,0:T(8,128)(2,1)S(1)}, bf16[1152,1152]{1,0:T(8,128)(2,1)}, u32[]{:S(2)}) copy-start(bf16[1152,1152]{1,0:T(8,128)(2,1)} %wo_ref.2) | copy-start | bytes 7962628
  66.6 26.2 %copy-start.2 = (bf16[1152,1152]{1,0:T(8,128)(2,1)S(1)}, bf16[1152,1152]{1,0:T(8,128)(2,1)}, u32[]{:S(2)}) copy-start(bf16[1152,1152]{1,0:T(8,128)(2,1)} %wo_ref.3) | copy-start | bytes 7962628
